TPU v7x, 256 devices: a whole 4x4x8 slice. The times are simulated.
256 devices in a mesh: seq: 32 (over z, y_lo, core), fsdp: 8 (over y_hi, x).
Axes of the slice: x: 4, y: 4 (y_hi: 2, y_lo: 2; y = y_hi * 2 + y_lo), z: 8, core: 2. Of those that a mesh axis runs over, the one named last changes fastest.
Arguments:
- queries: bfloat16 [16, 2048, 4096], P('fsdp', 'seq'), may hold values from -6 to 6
- key_rows: bfloat16 [16, 2048, 4096], P('fsdp', 'seq'), may hold values from -6 to 6
- value_rows: bfloat16 [16, 2048, 4096], P('fsdp', 'seq'), may hold values from -6 to 6
- query_tan: bfloat16 [16, 2048, 4096], P('fsdp', 'seq'), may hold values from -6 to 6
- key_tan: bfloat16 [16, 2048, 4096], P('fsdp', 'seq'), may hold values from -6 to 6
- value_tan: bfloat16 [16, 2048, 4096], P('fsdp', 'seq'), may hold values from -6 to 6
- residual: bfloat16 [16, 2048, 2560], P('fsdp', 'seq'), may hold values from -4 to 4
- residual_tan: bfloat16 [16, 2048, 2560], P('fsdp', 'seq'), may hold values from -6 to 6
- cond_mask: int32 [16, 2048], P('fsdp', 'seq'), may hold values 0 or 1
- time_index: int32 [16], P('fsdp'), may hold values from 0 to 63
- gate_table: float32 [64, 2560], replicated, may hold values from 0.5 to 1.5
- gate_slope: float32 [64, 2560], replicated, may hold values from -1 to 1
- out_weight: bfloat16 [4096, 2560], P(('seq', 'fsdp')), may hold values from -0.75 to 0.75
Outputs:
- block_out: bfloat16 [16, 2048, 2560], P('fsdp', 'seq')
- block_tan: bfloat16 [16, 2048, 2560], P('fsdp', 'seq')
All inputs are finite; a program needn't handle non-finite values. No bound on the sum of `cond_mask` on one device may be relied on, other than what follows from the above.
Results may differ from a plain program's by a relative error of at most 0.0057.
Values may be sent and summed in bfloat16 or wider, within the bound.
A program may use at most 128 MiB of HBM per device.

v0:
```python
import math

import jax
import jax.numpy as jnp
from jax import lax
from jax.sharding import PartitionSpec as P

HEAD_DIM = 128


def head_attention(tensors):
    query_head, key_head, value_head, query_dot, key_dot, value_dot = tensors
    length = query_head.shape[0]
    block_rows = math.gcd(length, 512)
    score_scale = HEAD_DIM ** (-0.5)
    keys_paired = jnp.concatenate([key_head, key_dot], -1)
    values_paired = jnp.concatenate([value_head, value_dot], -1)
    block_pairs = (
        query_head.reshape(length // block_rows, block_rows, HEAD_DIM),
        query_dot.reshape(length // block_rows, block_rows, HEAD_DIM),
    )

    def one_block(block_pair):
        query_blk, query_blk_dot = block_pair
        scores = jnp.dot(query_blk, key_head.T, preferred_element_type=jnp.float32) * score_scale
        queries_paired = jnp.concatenate([query_blk_dot, query_blk], -1)
        score_tan = (
            jnp.dot(queries_paired, keys_paired.T, preferred_element_type=jnp.float32) * score_scale
        )
        row_peak = jnp.max(scores, -1, keepdims=True)
        shifted_exp = jnp.exp(scores - row_peak)
        softmax = shifted_exp / jnp.sum(shifted_exp, -1, keepdims=True)
        softmax_low = softmax.astype(jnp.bfloat16)
        centre = jnp.sum(softmax * score_tan, -1, keepdims=True)
        weight_tan = (softmax * (score_tan - centre)).astype(jnp.bfloat16)
        both_values = jnp.dot(softmax_low, values_paired, preferred_element_type=jnp.float32)
        attended = both_values[:, :HEAD_DIM]
        attended_tan = both_values[:, HEAD_DIM:] + jnp.dot(
            weight_tan, value_head, preferred_element_type=jnp.float32
        )
        return (attended.astype(jnp.bfloat16), attended_tan.astype(jnp.bfloat16))

    outputs, tangents = lax.map(one_block, block_pairs)
    return (outputs.reshape(length, HEAD_DIM), tangents.reshape(length, HEAD_DIM))


def heads_work(parts):
    clip_count, length, _, head_count, head_dim = parts[0].shape

    def heads_first(array):
        return (
            array[:, :, 0].transpose(0, 2, 1, 3).reshape(clip_count * head_count, length, head_dim)
        )

    outputs, tangents = lax.map(head_attention, tuple((heads_first(array) for array in parts)))

    def tokens_back(array):
        return array.reshape(clip_count, head_count, length, head_dim).transpose(0, 2, 1, 3)[
            :, :, None
        ]

    return (tokens_back(outputs), tokens_back(tangents))


def body(
    queries,
    key_rows,
    value_rows,
    query_tan,
    key_tan,
    value_tan,
    residual,
    residual_tan,
    cond_mask,
    time_index,
    gate_table,
    gate_slope,
    out_weight,
):
    clip_count = queries.shape[0]
    tok_rows = queries.shape[1]
    width_all = queries.shape[2]
    seq_count = lax.axis_size("seq")
    head_count = width_all // (HEAD_DIM * seq_count)
    live = (cond_mask == 0)[..., None]
    nothing = jnp.zeros((), jnp.bfloat16)
    query_live = jnp.where(live, query_tan, nothing)
    key_live = jnp.where(live, key_tan, nothing)
    value_live = jnp.where(live, value_tan, nothing)

    def grouped(array):
        return array.reshape(clip_count, tok_rows, seq_count, head_count, HEAD_DIM)

    spread = (
        lax.all_to_all(grouped(queries), "seq", split_axis=2, concat_axis=1, tiled=True),
        lax.all_to_all(grouped(key_rows), "seq", split_axis=2, concat_axis=1, tiled=True),
        lax.all_to_all(grouped(value_rows), "seq", split_axis=2, concat_axis=1, tiled=True),
        lax.all_to_all(grouped(query_live), "seq", split_axis=2, concat_axis=1, tiled=True),
        lax.all_to_all(grouped(key_live), "seq", split_axis=2, concat_axis=1, tiled=True),
        lax.all_to_all(grouped(value_live), "seq", split_axis=2, concat_axis=1, tiled=True),
    )
    outputs, tangents = heads_work(spread)
    outputs, tangents = (
        lax.all_to_all(outputs, "seq", split_axis=1, concat_axis=2, tiled=True),
        lax.all_to_all(tangents, "seq", split_axis=1, concat_axis=2, tiled=True),
    )
    tokens_out = outputs.reshape(clip_count * tok_rows, width_all)
    tokens_tan = tangents.reshape(clip_count * tok_rows, width_all)
    out_width = out_weight.shape[1]
    whole_weight = lax.all_gather(out_weight, ("seq", "fsdp"), axis=0, tiled=True)
    projected = jnp.dot(tokens_out, whole_weight, preferred_element_type=jnp.float32)
    projected_tan = jnp.dot(tokens_tan, whole_weight, preferred_element_type=jnp.float32)
    projected = projected.reshape(clip_count, tok_rows, out_width)
    projected_tan = projected_tan.reshape(clip_count, tok_rows, out_width)
    selector = (lax.iota(jnp.int32, gate_table.shape[0])[None, :] == time_index[:, None]).astype(
        jnp.float32
    )
    gate = jnp.sum(gate_table[None] * selector[:, :, None], 1)[:, None, :]
    slope = jnp.sum(gate_slope[None] * selector[:, :, None], 1)[:, None, :]
    block_out = (residual.astype(jnp.float32) + gate * projected).astype(jnp.bfloat16)
    kept_tan = jnp.where(live, residual_tan, nothing).astype(jnp.float32)
    block_tan = (kept_tan + slope * projected + gate * projected_tan).astype(jnp.bfloat16)
    return (block_out, block_tan)


def solution(mesh):
    in_specs = (
        P("fsdp", "seq", None),
        P("fsdp", "seq", None),
        P("fsdp", "seq", None),
        P("fsdp", "seq", None),
        P("fsdp", "seq", None),
        P("fsdp", "seq", None),
        P("fsdp", "seq", None),
        P("fsdp", "seq", None),
        P("fsdp", "seq"),
        P("fsdp"),
        P(),
        P(),
        P(("seq", "fsdp"), None),
    )
    out_specs = (P("fsdp", "seq", None), P("fsdp", "seq", None))
    return jax.shard_map(body, mesh=mesh, in_specs=in_specs, out_specs=out_specs, check_vma=False)
```

profile of v0, /device:TPU:1, one launch (start us, length us, event | category | flops | bytes accessed | tf_op | source)
XLA Modules:
  0.0 924.5 jit_solution(11031842010255442356)
XLA Ops:
  7.8 2.1 broadcast_select_fusion
  11.6 11.1 %all-to-all-start.1 = ((bf16[2,64,32,1,128]{4,1,0,3,2:T(8,128)(2,1)}), bf16[2,64,32,1,128]{4,1,0,3,2:T(8,128)(2,1)S(1)}, u32[]{:S(2)}, u32[]{:S(2)}) async-start(bf16[2,64,32,1,128]{4,1,0,3,2:T(8,128)(2,1)} %copy.45), calls=%async_computation.1 | async-start | bytes 2097152 | tf_op jit(solution)/shard_map/all_to_all | solution.py:98
  24.4 26.5 %all-to-all-done.1 = bf16[2,64,32,1,128]{4,1,0,3,2:T(8,128)(2,1)S(1)} async-done(((bf16[2,64,32,1,128]{4,1,0,3,2:T(8,128)(2,1)}), bf16[2,64,32,1,128]{4,1,0,3,2:T(8,128)(2,1)S(1)}, u32[]{:S(2)}, u32[]{:S(2)}) %all-to-all-start.1) | async-done | bytes 1048608 | tf_op jit(solution)/shard_map/all_to_all | solution.py:98
  50.9 4.8 all-to-all-start.3
  57.3 26.6 %all-to-all-done.3 = bf16[2,64,32,1,128]{4,1,0,3,2:T(8,128)(2,1)S(1)} async-done(((bf16[2,64,32,1,128]{4,1,0,3,2:T(8,128)(2,1)}), bf16[2,64,32,1,128]{4,1,0,3,2:T(8,128)(2,1)S(1)}, u32[]{:S(2)}, u32[]{:S(2)}) %all-to-all-start.3) | async-done | bytes 1048608 | tf_op jit(solution)/shard_map/all_to_all | solution.py:99
  83.9 5.0 all-to-all-start.5
  91.7 25.3 %all-to-all-done.5 = bf16[2,64,32,1,128]{4,1,0,3,2:T(8,128)(2,1)S(1)} async-done(((bf16[2,64,32,1,128]{4,1,0,3,2:T(8,128)(2,1)}), bf16[2,64,32,1,128]{4,1,0,3,2:T(8,128)(2,1)S(1)}, u32[]{:S(2)}, u32[]{:S(2)}) %all-to-all-start.5) | async-done | bytes 1048608 | tf_op jit(solution)/shard_map/all_to_all | solution.py:100
  117.1 5.6 all-to-all-start
  126.3 26.4 %all-to-all-done = bf16[2,64,32,1,128]{4,1,0,3,2:T(8,128)(2,1)} async-done(((bf16[2,64,32,1,128]{4,1,0,3,2:T(8,128)(2,1)}), bf16[2,64,32,1,128]{4,1,0,3,2:T(8,128)(2,1)}, u32[]{:S(2)}, u32[]{:S(2)}) %all-to-all-start) | async-done | bytes 1048608 | tf_op jit(solution)/shard_map/all_to_all | solution.py:95
  152.7 5.1 all-to-all-start.2
  160.6 29.2 %all-to-all-done.2 = bf16[2,64,32,1,128]{4,1,0,3,2:T(8,128)(2,1)} async-done(((bf16[2,64,32,1,128]{4,1,0,3,2:T(8,128)(2,1)}), bf16[2,64,32,1,128]{4,1,0,3,2:T(8,128)(2,1)}, u32[]{:S(2)}, u32[]{:S(2)}) %all-to-all-start.2) | async-done | bytes 1048608 | tf_op jit(solution)/shard_map/all_to_all | solution.py:96
  189.8 4.7 all-to-all-start.4
  197.8 2.3 copy.44
  200.1 2.4 copy.48
  202.4 23.4 %all-to-all-done.4 = bf16[2,64,32,1,128]{4,1,0,3,2:T(8,128)(2,1)} async-done(((bf16[2,64,32,1,128]{4,1,0,3,2:T(8,128)(2,1)}), bf16[2,64,32,1,128]{4,1,0,3,2:T(8,128)(2,1)}, u32[]{:S(2)}, u32[]{:S(2)}) %all-to-all-start.4) | async-done | bytes 1048608 | tf_op jit(solution)/shard_map/all_to_all | solution.py:97
  225.8 2.3 copy.52
  228.1 81.9 %while.25 = (s32[]{:T(128)}, bf16[2,2048,128]{2,1,0:T(8,128)(2,1)}, bf16[2,2048,128]{2,1,0:T(8,128)(2,1)}, bf16[2,2048,128]{2,1,0:T(8,128)(2,1)}, bf16[2,2048,12...) while((s32[]{:T(128)}, bf16[2,2048,128]{2,1,0:T(8,128)(2,1)}, ...), condition=%wide.region_7.8_spmd, body=%wide.region_1.7_spmd.sunk | while | flops 1638529536 | bytes 59793312 | solution.py:55
  234.0 32.8 %while.26 = (s32[]{:T(128)}, bf16[4,512,128]{2,1,0:T(8,128)(2,1)}, bf16[4,512,128]{2,1,0:T(8,128)(2,1)}, bf16[4,512,128]{2,1,0:T(8,128)(2,1)S(1)}, bf16[2048,128...) while((s32[]{:T(128)}, bf16[4,512,128]{2,1,0:T(8,128)(2,1)}, ...), condition=%wide.region_6.6_spmd, body=%wide.region_2.5_spmd.sunk | while | flops 1634335232 | bytes 38820996 | solution.py:43
  235.7 1.9 multiply_reduce_fusion.7
  238.9 2.6 fusion.62
  243.9 1.9 multiply_reduce_fusion.7
  247.1 2.6 fusion.62
  252.0 1.9 multiply_reduce_fusion.7
  255.3 2.6 fusion.62
  260.2 1.9 multiply_reduce_fusion.7
  263.5 2.6 fusion.62
  266.8 2.2 bitcast_dynamic-update-slice_fusion.3
  274.9 32.8 %while.26 = (s32[]{:T(128)}, bf16[4,512,128]{2,1,0:T(8,128)(2,1)}, bf16[4,512,128]{2,1,0:T(8,128)(2,1)}, bf16[4,512,128]{2,1,0:T(8,128)(2,1)S(1)}, bf16[2048,128...) while((s32[]{:T(128)}, bf16[4,512,128]{2,1,0:T(8,128)(2,1)}, ...), condition=%wide.region_6.6_spmd, body=%wide.region_2.5_spmd.sunk | while | flops 1634335232 | bytes 38820996 | solution.py:43
  276.6 1.9 multiply_reduce_fusion.7
  279.9 2.6 fusion.62
  284.8 1.9 multiply_reduce_fusion.7
  288.1 2.6 fusion.62
  293.0 1.9 multiply_reduce_fusion.7
  296.3 2.6 fusion.62
  301.2 1.9 multiply_reduce_fusion.7
  304.5 2.6 fusion.62
  307.7 2.3 bitcast_dynamic-update-slice_fusion.3
  310.0 3.7 copy.72
  313.7 4.7 all-to-all-start.6
  318.5 9.5 %copy.70 = bf16[2,2048,128]{2,0,1:T(2,128)(2,1)} copy(bf16[2,2048,128]{2,1,0:T(8,128)(2,1)S(1)} %copy-done.4) | data formatting | bytes 2097152 | tf_op jit(solution)/shard_map/while | solution.py:55
  328.0 21.4 %all-to-all-done.6 = bf16[2,2048,1,1,128]{4,0,3,2,1:T(2,128)(2,1)S(1)} async-done(((bf16[2,2048,1,1,128]{4,0,3,2,1:T(2,128)(2,1)}), bf16[2,2048,1,1,128]{4,0,3,2,1:T(2,128)(2,1)S(1)}, u32[]{:S(2)}, u32[]{:S(2)}) %all-to-all-start.6) | async-done | bytes 1048608 | tf_op jit(solution)/shard_map/all_to_all | solution.py:104
  349.3 5.1 all-to-all-start.7
  356.0 29.0 %all-to-all-done.7 = bf16[2,2048,1,1,128]{4,0,3,2,1:T(2,128)(2,1)S(1)} async-done(((bf16[2,2048,1,1,128]{4,0,3,2,1:T(2,128)(2,1)}), bf16[2,2048,1,1,128]{4,0,3,2,1:T(2,128)(2,1)S(1)}, u32[]{:S(2)}, u32[]{:S(2)}) %all-to-all-start.7) | async-done | bytes 1048608 | tf_op jit(solution)/shard_map/all_to_all | solution.py:105
  386.1 510.6 %all-gather.2.cloned.1.call-done = bf16[4096,2560]{1,0:T(8,128)(2,1)} async-done(((bf16[16,2560]{1,0:T(8,128)(2,1)}), bf16[4096,2560]{1,0:T(8,128)(2,1)}) %all-gather.2.cloned.1.call-update) | async-done | bytes 20971536 | tf_op jit(solution)/shard_map/all_gather | solution.py:110
  896.8 8.7 fusion.29
  905.5 4.2 copy-done
  909.7 5.4 add_convert_fusion
  915.1 2.6 fusion.32
  (125 shorter events, 61.9 us)
Async XLA Ops:
  7.8 2.4 copy-start.8
  11.6 39.3 %all-to-all-start.1 = ((bf16[2,64,32,1,128]{4,1,0,3,2:T(8,128)(2,1)}), bf16[2,64,32,1,128]{4,1,0,3,2:T(8,128)(2,1)S(1)}, u32[]{:S(2)}, u32[]{:S(2)}) async-start(bf16[2,64,32,1,128]{4,1,0,3,2:T(8,128)(2,1)} %copy.45), calls=%async_computation.1 | async-start | bytes 2097152 | tf_op jit(solution)/shard_map/all_to_all | solution.py:98
  50.9 33.0 %all-to-all-start.3 = ((bf16[2,64,32,1,128]{4,1,0,3,2:T(8,128)(2,1)}), bf16[2,64,32,1,128]{4,1,0,3,2:T(8,128)(2,1)S(1)}, u32[]{:S(2)}, u32[]{:S(2)}) async-start(bf16[2,64,32,1,128]{4,1,0,3,2:T(8,128)(2,1)} %copy.49), calls=%async_computation.3 | async-start | bytes 2097152 | tf_op jit(solution)/shard_map/all_to_all | solution.py:99
  83.9 33.2 %all-to-all-start.5 = ((bf16[2,64,32,1,128]{4,1,0,3,2:T(8,128)(2,1)}), bf16[2,64,32,1,128]{4,1,0,3,2:T(8,128)(2,1)S(1)}, u32[]{:S(2)}, u32[]{:S(2)}) async-start(bf16[2,64,32,1,128]{4,1,0,3,2:T(8,128)(2,1)} %copy.53), calls=%async_computation.5 | async-start | bytes 2097152 | tf_op jit(solution)/shard_map/all_to_all | solution.py:100
  117.1 35.6 %all-to-all-start = ((bf16[2,64,32,1,128]{4,1,0,3,2:T(8,128)(2,1)}), bf16[2,64,32,1,128]{4,1,0,3,2:T(8,128)(2,1)}, u32[]{:S(2)}, u32[]{:S(2)}) async-start(bf16[2,64,32,1,128]{4,1,0,3,2:T(8,128)(2,1)} %copy.43), calls=%async_computation | async-start | bytes 2097152 | tf_op jit(solution)/shard_map/all_to_all | solution.py:95
  122.7 774.1 %all-gather.2.cloned.1.call-start = ((), (), s32[]{:S(2)}) async-start(), calls=%async_computation.8 | async-start | bytes 21053440 | tf_op jit(solution)/shard_map/all_gather | solution.py:110
  152.7 37.2 %all-to-all-start.2 = ((bf16[2,64,32,1,128]{4,1,0,3,2:T(8,128)(2,1)}), bf16[2,64,32,1,128]{4,1,0,3,2:T(8,128)(2,1)}, u32[]{:S(2)}, u32[]{:S(2)}) async-start(bf16[2,64,32,1,128]{4,1,0,3,2:T(8,128)(2,1)} %copy.47), calls=%async_computation.2 | async-start | bytes 2097152 | tf_op jit(solution)/shard_map/all_to_all | solution.py:96
  189.8 35.9 %all-to-all-start.4 = ((bf16[2,64,32,1,128]{4,1,0,3,2:T(8,128)(2,1)}), bf16[2,64,32,1,128]{4,1,0,3,2:T(8,128)(2,1)}, u32[]{:S(2)}, u32[]{:S(2)}) async-start(bf16[2,64,32,1,128]{4,1,0,3,2:T(8,128)(2,1)} %copy.51), calls=%async_computation.4 | async-start | bytes 2097152 | tf_op jit(solution)/shard_map/all_to_all | solution.py:97
  228.1 5.8 copy-start.3
  229.2 4.7 copy-start.2
  234.0 1.6 copy-start.1
  242.2 1.6 copy-start.1
  250.4 1.6 copy-start.1
  258.6 1.6 copy-start.1
  269.0 5.8 copy-start.3
  270.2 4.7 copy-start.2
  275.0 1.6 copy-start.1
  283.2 1.6 copy-start.1
  291.4 1.6 copy-start.1
  299.6 1.6 copy-start.1
  310.0 8.5 copy-start.4
  310.0 44.5 %copy-start.10 = (s32[2]{0:T(128)S(1)}, s32[2]{0:T(128)}, u32[]{:S(2)}) copy-start(s32[2]{0:T(128)} %param.26) | copy-start | bytes 28
  310.0 44.6 %copy-start.5 = (f32[64,2560]{1,0:T(8,128)S(1)}, f32[64,2560]{1,0:T(8,128)}, u32[]{:S(2)}) copy-start(f32[64,2560]{1,0:T(8,128)} %param.27) | copy-start | bytes 1966084
  313.7 35.6 %all-to-all-start.6 = ((bf16[2,2048,1,1,128]{4,0,3,2,1:T(2,128)(2,1)}), bf16[2,2048,1,1,128]{4,0,3,2,1:T(2,128)(2,1)S(1)}, u32[]{:S(2)}, u32[]{:S(2)}) async-start(bf16[2,2048,1,1,128]{4,0,3,2,1:T(2,128)(2,1)} %bitcast.124), calls=%async_computation.6 | async-start | bytes 2097152 | tf_op jit(solution)/shard_map/all_to_all | solution.py:104
  349.3 35.6 %all-to-all-start.7 = ((bf16[2,2048,1,1,128]{4,0,3,2,1:T(2,128)(2,1)}), bf16[2,2048,1,1,128]{4,0,3,2,1:T(2,128)(2,1)S(1)}, u32[]{:S(2)}, u32[]{:S(2)}) async-start(bf16[2,2048,1,1,128]{4,0,3,2,1:T(2,128)(2,1)} %bitcast.122), calls=%async_computation.7 | async-start | bytes 2097152 | tf_op jit(solution)/shard_map/all_to_all | solution.py:105
  896.8 12.9 %copy-start = (bf16[4096,2560]{1,0:T(8,128)(2,1)S(1)}, bf16[4096,2560]{1,0:T(8,128)(2,1)}, u32[]{:S(2)}) copy-start(bf16[4096,2560]{1,0:T(8,128)(2,1)} %all-gather.2.cloned.1.call-done) | copy-start | bytes 62914564
  909.7 5.4 copy-start.6
  909.7 5.4 copy-start.7
  909.7 5.4 copy-start.9
Sparse Core Ops, SparseCore 0:
  125.4 771.3 all-gather.1
where the time goes:
time: 933 us; the launch traced here: 924 us
  waiting for transfers between devices  719 us (77%)
  matrix products  67.2 us (7%)
  local copies, waits for them, and re-layouts  62.7 us (7%)
  starting transfers between devices  46.2 us (5%)
  other arithmetic  14.8 us (2%)
  between operations  14.2 us (2%)
    all_gather x1, waiting for transfers between devices, body(): lax.all_gather(out_weight, ('seq', 'fsdp'), axis=0, tiled=True)  511 us
    all_to_all x1, waiting for transfers between devices, body(): lax.all_to_all(grouped(key_rows), 'seq', split_axis=2, concat_axis=1, til...  29.2 us
    all_to_all x1, waiting for transfers between devices, body(): lax.all_to_all(tangents, 'seq', split_axis=1, concat_axis=2, tiled=True)  29 us
    all_to_all x1, waiting for transfers between devices, body(): lax.all_to_all(grouped(key_live), 'seq', split_axis=2, concat_axis=1, til...  26.6 us
    all_to_all x1, waiting for transfers between devices, body(): lax.all_to_all(grouped(query_live), 'seq', split_axis=2, concat_axis=1, t...  26.5 us
    all_to_all x1, waiting for transfers between devices, body(): lax.all_to_all(grouped(queries), 'seq', split_axis=2, concat_axis=1, tile...  26.4 us
    all_to_all x1, waiting for transfers between devices, body(): lax.all_to_all(grouped(value_live), 'seq', split_axis=2, concat_axis=1, t...  25.3 us
    all_to_all x1, waiting for transfers between devices, body(): lax.all_to_all(grouped(value_rows), 'seq', split_axis=2, concat_axis=1, t...  23.4 us
  transfers between devices with their start and end apart: 9, of which 9 were waited for; matrix products, arithmetic and copies ran while one was open for 13% of the time, Pallas kernels for 0%

commit v1 on v0

v1 whole, which is shorter than its diff:
```python
import functools
import math

import jax
import jax.numpy as jnp
from jax import lax
from jax.experimental import pallas as pl
from jax.experimental.pallas import tpu as pltpu
from jax.sharding import PartitionSpec as P

HEAD_DIM = 128
Y_LO, CORE, Y_HI = 2, 2, 2
GROUP = Y_LO * CORE
CLIPS = 2
NARROW = jnp.bfloat16
WIDE = jnp.float32


def column_of(row, length):
    square = (length, length)
    same = lax.broadcasted_iota(jnp.int32, square, 0) == lax.broadcasted_iota(jnp.int32, square, 1)
    return jnp.sum(jnp.where(same, jnp.broadcast_to(row, square), 0.0), 1, keepdims=True)


def kernel(
    dims,
    q_ref, k_ref, v_ref, qt_ref, kt_ref, vt_ref, res_ref, rest_ref,
    mask_ref, time_ref, gate_ref, slope_ref, weight_ref,
    out_ref, tan_ref,
    raw, kvsend, kvbuf, qsend, qbuf, osend, orecv, wbuf, resbuf, gatebuf,
    scores, probs, sums, joined,
    load_sem, res_sem, kv_ss, kv_rs, q_ss, q_rs, o_ss, o_rs, w_ss, w_rs, own_sem,
):
    n_z, n_x, tok, n_out = dims
    n_seq = n_z * GROUP
    length = n_seq * tok
    d = HEAD_DIM
    rows = GROUP * tok
    me = lax.axis_index("seq")
    my_f = lax.axis_index("fsdp")
    z, y_lo, core = me // GROUP, (me // CORE) % Y_LO, me % CORE
    y_hi, x = my_f // n_x, my_f % n_x
    y_hi_count = dims_y_hi(dims)

    def seq_peer(slot, sign):
        ring = slot // GROUP
        half = (ring + 1) // 2
        dz = (2 * (ring % 2) - 1) * half * sign
        pz = (z + dz + n_z) % n_z
        py = (y_lo + (slot // CORE) % Y_LO) % Y_LO
        pc = (core + slot) % CORE
        return pz * GROUP + py * CORE + pc

    def device(seq, fsdp):
        return {"seq": seq, "fsdp": fsdp}

    x_peers = [device(me, y_hi * n_x + (x + dx) % n_x) for dx in range(1, n_x)]
    y_peers = [
        device(
            z * GROUP + ((y_lo + a) % Y_LO) * CORE + core,
            ((y_hi + b) % y_hi_count) * n_x + x,
        )
        for b in range(y_hi_count)
        for a in range(Y_LO)
        if (a, b) != (0, 0)
    ]
    y_far = [p for p, (b, a) in zip(
        y_peers,
        [(b, a) for b in range(y_hi_count) for a in range(Y_LO) if (a, b) != (0, 0)],
    ) if b]

    streams = (k_ref, kt_ref, v_ref, vt_ref, qt_ref, q_ref)

    def load(clip, stream):
        return pltpu.make_async_copy(
            streams[stream].at[clip], raw.at[clip, stream], load_sem.at[clip, stream]
        )

    for clip in range(CLIPS):
        for stream in range(6):
            load(clip, stream).start()
    own_weight = pltpu.make_async_copy(weight_ref, wbuf.at[z, y_lo, core, y_hi, x], own_sem.at[0])
    own_weight.start()
    late_loads = [
        pltpu.make_async_copy(res_ref, resbuf.at[0], res_sem.at[0]),
        pltpu.make_async_copy(rest_ref, resbuf.at[1], res_sem.at[1]),
        pltpu.make_async_copy(gate_ref, gatebuf.at[0], res_sem.at[2]),
        pltpu.make_async_copy(slope_ref, gatebuf.at[1], res_sem.at[3]),
    ]

    barrier = pltpu.get_barrier_semaphore()

    def greet(slot, carry):
        pl.semaphore_signal(barrier, inc=1, device_id=device(seq_peer(slot, 1), my_f))
        return carry

    lax.fori_loop(1, n_seq, greet, 0)
    for peer in x_peers + y_far:
        pl.semaphore_signal(barrier, inc=1, device_id=peer)

    live = [
        column_of((mask_ref[pl.ds(clip, 1), :] == 0).astype(WIDE), tok) for clip in range(CLIPS)
    ]

    def pack_kv(clip):
        for stream in range(4):
            load(clip, stream).wait()

        def one(head, carry):
            lanes = pl.ds(pl.multiple_of(head * d, d), d)
            for stream in range(4):
                part = raw[clip, stream, :, lanes]
                if stream % 2:
                    part = (part.astype(WIDE) * live[clip]).astype(NARROW)
                kvsend[clip, head, :, stream * d : (stream + 1) * d] = part
            return carry

        lax.fori_loop(0, n_seq, one, 0)

    def pack_q(clip):
        for stream in range(4, 6):
            load(clip, stream).wait()

        def one(head, carry):
            lanes = pl.ds(pl.multiple_of(head * d, d), d)
            part = raw[clip, 4, :, lanes]
            qsend[clip, head, :, :d] = (part.astype(WIDE) * live[clip]).astype(NARROW)
            qsend[clip, head, :, d:] = raw[clip, 5, :, lanes]
            return carry

        lax.fori_loop(0, n_seq, one, 0)

    def send_kv(clip):
        def one(slot, carry):
            peer = seq_peer(slot, 1)
            pltpu.make_async_remote_copy(
                src_ref=kvsend.at[clip, peer],
                dst_ref=kvbuf.at[clip, pl.ds(pl.multiple_of(slot * tok, tok), tok)],
                send_sem=kv_ss.at[clip],
                recv_sem=kv_rs.at[clip],
                device_id=device(peer, my_f),
            ).start()
            return carry

        lax.fori_loop(1, n_seq, one, 0)
        kvbuf[clip, :tok] = kvsend[clip, me]

    def send_q(clip):
        def one(slot, carry):
            peer = seq_peer(slot, 1)
            pltpu.make_async_remote_copy(
                src_ref=qsend.at[clip, peer],
                dst_ref=qbuf.at[clip, pl.ds(pl.multiple_of(slot * tok, tok), tok)],
                send_sem=q_ss.at[clip],
                recv_sem=q_rs.at[clip, slot // GROUP],
                device_id=device(peer, my_f),
            ).start()
            return carry

        lax.fori_loop(1, n_seq, one, 0)
        qbuf[clip, :tok] = qsend[clip, me]

    def drain(ref, sem):
        pltpu.make_async_copy(ref, ref, sem).wait()

    pack_kv(0)
    pl.semaphore_wait(barrier, n_seq - 1 + len(x_peers) + len(y_far))

    own_weight.wait()
    mine = wbuf.at[z, y_lo, core, y_hi, x]

    def spread_z(step, carry):
        peer_z = (z + step) % n_z
        pltpu.make_async_remote_copy(
            src_ref=mine, dst_ref=mine, send_sem=w_ss.at[0], recv_sem=w_rs.at[0],
            device_id=device(peer_z * GROUP + y_lo * CORE + core, my_f),
        ).start()
        return carry

    lax.fori_loop(1, n_z, spread_z, 0)
    send_kv(0)
    pack_q(0)
    send_q(0)
    pack_kv(1)
    send_kv(1)
    pack_q(1)
    send_q(1)
    for copy in late_loads:
        copy.start()

    drain(wbuf.at[: n_z - 1, 0, 0, 0, 0], w_rs.at[0])
    for peer in y_peers:
        part = wbuf.at[:, y_lo, core, y_hi, x]
        pltpu.make_async_remote_copy(
            src_ref=part, dst_ref=part, send_sem=w_ss.at[1], recv_sem=w_rs.at[1], device_id=peer
        ).start()
    drain(wbuf.at[:, 0, 0, 0, : len(y_peers)], w_rs.at[1])
    for peer in x_peers:
        part = wbuf.at[:, :, core, :, x]
        pltpu.make_async_remote_copy(
            src_ref=part, dst_ref=part, send_sem=w_ss.at[2], recv_sem=w_rs.at[2], device_id=peer
        ).start()

    scale = d ** (-0.5)
    to_exponent = scale * math.log2(math.e)
    step_rows = 16

    def attend(clip):
        drain(kvbuf.at[clip, tok:], kv_rs.at[clip])

        def block(index, carry):
            start = pl.multiple_of(index * rows, rows)

            @pl.when(index == 0)
            def _():
                drain(qbuf.at[clip, tok:rows], q_rs.at[clip, 0])

            @pl.when(index != 0)
            def _():
                drain(qbuf.at[clip, pl.ds(start, rows)], q_rs.at[clip, index])

            both = qbuf[clip, pl.ds(start, rows)]
            plain = both[:, d:]
            left = jnp.concatenate(
                [jnp.concatenate([plain, jnp.zeros_like(plain)], 1), both], 0
            )
            scores[...] = lax.dot_general(
                left, kvbuf[clip, :, : 2 * d], (((1,), (1,)), ((), ())),
                preferred_element_type=WIDE,
            )

            def soften(step, carry):
                at = pl.multiple_of(step * step_rows, step_rows)
                exponent = scores[pl.ds(at, step_rows)] * to_exponent
                weight = jnp.exp2(exponent - jnp.max(exponent, 1, keepdims=True))
                total = jnp.sum(weight, 1, keepdims=True)
                slant = scores[pl.ds(rows + at, step_rows)]
                centre = jnp.sum(weight * slant, 1, keepdims=True) / total
                probs[pl.ds(at, step_rows)] = weight.astype(NARROW)
                probs[pl.ds(rows + at, step_rows)] = (weight * (slant - centre)).astype(NARROW)
                sums[pl.ds(at, step_rows)] = jnp.broadcast_to(1.0 / total, (step_rows, d))
                return carry

            lax.fori_loop(0, rows // step_rows, soften, 0)
            result = jnp.dot(
                probs[...], kvbuf[clip, :, 2 * d :], preferred_element_type=WIDE
            )
            inverse = sums[...]
            value = (result[:rows, :d] * inverse).astype(NARROW)
            value_tan = (
                (result[rows:, :d] * scale + result[:rows, d:]) * inverse
            ).astype(NARROW)
            for part in range(GROUP):
                slot = index * GROUP + part
                at = slice(part * tok, (part + 1) * tok)
                osend[clip, slot, :tok] = value[at]
                osend[clip, slot, tok:] = value_tan[at]
            for part in range(GROUP):
                slot = index * GROUP + part
                copy = pltpu.make_async_remote_copy(
                    src_ref=osend.at[clip, slot],
                    dst_ref=orecv.at[clip, me],
                    send_sem=o_ss.at[clip],
                    recv_sem=o_rs.at[clip],
                    device_id=device(seq_peer(slot, -1), my_f),
                )
                if part:
                    copy.start()
                else:
                    pl.when(index != 0)(copy.start)
            return carry

        lax.fori_loop(0, n_z, block, 0)
        orecv[clip, me] = osend[clip, 0]

    attend(0)
    drain(wbuf.at[:, :, 0, :, : n_x - 1], w_rs.at[2])
    part = wbuf.at[:, :, core]
    pltpu.make_async_remote_copy(
        src_ref=part, dst_ref=part, send_sem=w_ss.at[3], recv_sem=w_rs.at[3],
        device_id=device(z * GROUP + y_lo * CORE + (core + 1) % CORE, my_f),
    ).start()
    attend(1)
    drain(wbuf.at[:, :, 0], w_rs.at[3])
    for copy in late_loads:
        copy.wait()

    tile = 256
    steps = gatebuf.shape[1]

    def project(clip):
        drain(orecv.at[clip, : n_seq - 1], o_rs.at[clip])
        for head in range(n_seq):
            joined[:, head * d : (head + 1) * d] = orecv[clip, head]
        picked = (
            lax.broadcasted_iota(jnp.int32, (steps, 1), 0) == time_ref[clip]
        ).astype(WIDE)

        def one(index, carry):
            lanes = pl.ds(pl.multiple_of(index * tile, tile), tile)
            weight = wbuf[:, :, :, :, :, :, lanes].reshape(n_seq * d, tile)
            both = jnp.dot(joined[...], weight, preferred_element_type=WIDE)
            gate = jnp.sum(gatebuf[0, :, lanes] * picked, 0, keepdims=True)
            slope = jnp.sum(gatebuf[1, :, lanes] * picked, 0, keepdims=True)
            plain, tangent = both[:tok], both[tok:]
            out_ref[clip, :, lanes] = (
                resbuf[0, clip, :, lanes].astype(WIDE) + gate * plain
            ).astype(NARROW)
            tan_ref[clip, :, lanes] = (
                resbuf[1, clip, :, lanes].astype(WIDE) * live[clip] + slope * plain + gate * tangent
            ).astype(NARROW)
            return carry

        lax.fori_loop(0, n_out // tile, one, 0)

    project(0)
    project(1)

    for clip in range(CLIPS):
        drain(kvsend.at[clip, : n_seq - 1], kv_ss.at[clip])
        drain(qsend.at[clip, : n_seq - 1], q_ss.at[clip])
        drain(osend.at[clip, : n_seq - 1], o_ss.at[clip])
    drain(wbuf.at[: n_z - 1, 0, 0, 0, 0], w_ss.at[0])
    drain(wbuf.at[:, 0, 0, 0, : len(y_peers)], w_ss.at[1])
    drain(wbuf.at[:, :, 0, :, : n_x - 1], w_ss.at[2])
    drain(wbuf.at[:, :, 0], w_ss.at[3])


def dims_y_hi(dims):
    return Y_HI


def body(*args):
    (queries, key_rows, value_rows, query_tan, key_tan, value_tan, residual, residual_tan,
     cond_mask, time_index, gate_table, gate_slope, out_weight) = args
    clips, tok, width = queries.shape
    n_out = out_weight.shape[1]
    n_seq = lax.axis_size("seq")
    n_z = n_seq // GROUP
    n_x = lax.axis_size("fsdp") // Y_HI
    d = HEAD_DIM
    length = n_seq * tok
    rows = GROUP * tok
    steps = gate_table.shape[0]
    w_rows = out_weight.shape[0]
    anywhere = pl.BlockSpec(memory_space=pl.ANY)
    vmem = pl.BlockSpec(memory_space=pltpu.VMEM)
    smem = pl.BlockSpec(memory_space=pltpu.SMEM)
    out_shape = jax.ShapeDtypeStruct((clips, tok, n_out), NARROW)
    dma = pltpu.SemaphoreType.DMA
    return pl.pallas_call(
        functools.partial(kernel, (n_z, n_x, tok, n_out)),
        out_shape=(out_shape, out_shape),
        in_specs=[anywhere] * 8 + [vmem, smem] + [anywhere] * 3,
        out_specs=(vmem, vmem),
        scratch_shapes=[
            pltpu.VMEM((clips, 6, tok, width), NARROW),
            pltpu.VMEM((clips, n_seq, tok, 4 * d), NARROW),
            pltpu.VMEM((clips, length, 4 * d), NARROW),
            pltpu.VMEM((clips, n_seq, tok, 2 * d), NARROW),
            pltpu.VMEM((clips, length, 2 * d), NARROW),
            pltpu.VMEM((clips, n_seq, 2 * tok, d), NARROW),
            pltpu.VMEM((clips, n_seq, 2 * tok, d), NARROW),
            pltpu.VMEM((n_z, Y_LO, CORE, Y_HI, n_x, w_rows, n_out), NARROW),
            pltpu.VMEM((2, clips, tok, n_out), NARROW),
            pltpu.VMEM((2, steps, n_out), WIDE),
            pltpu.VMEM((2 * rows, length), WIDE),
            pltpu.VMEM((2 * rows, length), NARROW),
            pltpu.VMEM((rows, d), WIDE),
            pltpu.VMEM((2 * tok, width), NARROW),
            dma((clips, 6)), dma((4,)),
            dma((clips,)), dma((clips,)), dma((clips,)), dma((clips, n_z)), dma((clips,)), dma((clips,)),
            dma((4,)), dma((4,)), dma((1,)),
        ],
        compiler_params=pltpu.CompilerParams(
            collective_id=0, has_side_effects=True, vmem_limit_bytes=62 * 2**20
        ),
        cost_estimate=pl.CostEstimate(
            flops=20 * 10**9, bytes_accessed=12 * 2**20, transcendentals=8 * 2**20
        ),
    )(*args)


def solution(mesh):
    tokens = P("fsdp", "seq", None)
    in_specs = (tokens,) * 8 + (P("fsdp", "seq"), P("fsdp"), P(), P(), P(("seq", "fsdp"), None))
    return jax.shard_map(
        body, mesh=mesh, in_specs=in_specs, out_specs=(tokens, tokens), check_vma=False
    )
```

time: 933 us -> 265 us (0.28)
  waiting for transfers between devices: 719 us -> 0 us
  Pallas kernels: 0 us -> 262 us
  matrix products: 67.2 us -> 0 us
  local copies, waits for them, and re-layouts: 62.7 us -> 2.87 us
  starting transfers between devices: 46.2 us -> 0 us
  other arithmetic: 14.8 us -> 0 us
  between operations: 14.2 us -> 0.65 us
    all_gather x1 -> x0, waiting for transfers between devices: 511 us -> none  [body(): lax.all_gather(out_weight, ('seq', 'fsdp'), axis=0, tiled=True)]
    pallas_call x0 -> x1, Pallas kernels: none -> 262 us  [body(): pl.pallas_call(functools.partial(kernel, (n_z, n_x, tok, n_out)), out_sha...]
    all_to_all x8 -> x0, waiting for transfers between devices: 208 us -> none  [the longest x1 29.2 us: body(): lax.all_to_all(grouped(key_rows), 'seq', split_axis=2, concat_axis=1, til...]
    dot_general x34 -> x0, matrix products: 67.2 us -> none  [the longest x8 20.7 us: one_block(): jnp.dot(weight_tan, value_head, preferred_element_type=jnp.float32)]
    all_to_all x8 -> x0, starting transfers between devices: 46.1 us -> none  [the longest x1 11.1 us: body(): lax.all_to_all(grouped(query_live), 'seq', split_axis=2, concat_axis=1, t...]
    while x26 -> x0, local copies, waits for them, and re-layouts: 13.3 us -> none  [the longest x2 13.2 us: heads_work(): lax.map(head_attention, tuple((heads_first(array) for array in parts)))]
    all_to_all x8 -> x0, local copies, waits for them, and re-layouts: 11.6 us -> none  [the longest x1 2.36 us: body(): lax.all_to_all(grouped(key_rows), 'seq', split_axis=2, concat_axis=1, til...]
    dynamic_update_slice x10 -> x0, local copies, waits for them, and re-layouts: 9.88 us -> none  [the longest x8 5.38 us: head_attention(): outputs, tangents = lax.map(one_block, block_pairs)]
  transfers between devices with their start and end apart: 9 -> 0, of which waited for: 9 -> 0; matrix products, arithmetic and copies ran while one was open for 13% -> 0% of each run, Pallas kernels for 0% -> 0%
where the time goes in v1:
time: 265 us
  Pallas kernels  262 us (99%)
  local copies, waits for them, and re-layouts  2.87 us (1%)
    pallas_call x1, Pallas kernels, body(): pl.pallas_call(functools.partial(kernel, (n_z, n_x, tok, n_out)), out_sha...  262 us

profile of v1, /device:TPU:1, one launch (start us, length us, event | category | flops | bytes accessed | tf_op | source)
XLA Modules:
  0.0 265.3 jit_solution(6145304694180592187)
XLA Ops:
  0.6 261.7 %shard_map.140 = (bf16[2,64,2560]{2,1,0:T(8,128)(2,1)}, bf16[2,64,2560]{2,1,0:T(8,128)(2,1)}) custom-call(bf16[2,64,4096]{2,1,0:T(8,128)(2,1)} %q_ref.1, bf16[2,64,4096]{2,1,0:T(8,128)(2,1)} %k_ref.1, bf16[2,64,4096]{2,1,0:T(8,128)(2,1)} %v_ref.1, bf16[2,64,4096]{2,1,0:T(8,128)(2,1)} %qt_ref.1, bf16[2,64,4096]{2,1,0:T(8,128)(2,1)} %kt_ref.1, ...), custom_call_target="tpu_custom_call" | custom-call | flops 20000000000 | bytes 12582912 | tf_op jit(solution)/shard_map/pallas_call | solution.py:351
  262.4 0.0 copy-start
  262.4 2.0 copy.17
  264.4 0.0 copy-done
  264.4 0.8 copy.18
Async XLA Ops:
  262.4 2.0 copy-start

commit v2 on v1

--- a/solution.py
+++ b/solution.py
@@ -11,6 +11,7 @@
 HEAD_DIM = 128
 Y_LO, CORE, Y_HI = 2, 2, 2
 GROUP = Y_LO * CORE
+EARLY_CHUNKS = 6
 CLIPS = 2
 NARROW = jnp.bfloat16
 WIDE = jnp.float32
@@ -42,11 +43,11 @@
     y_hi, x = my_f // n_x, my_f % n_x
     y_hi_count = dims_y_hi(dims)
 
+    def ring_z(step, sign):
+        return (z + (2 * (step % 2) - 1) * ((step + 1) // 2) * sign + n_z) % n_z
+
     def seq_peer(slot, sign):
-        ring = slot // GROUP
-        half = (ring + 1) // 2
-        dz = (2 * (ring % 2) - 1) * half * sign
-        pz = (z + dz + n_z) % n_z
+        pz = ring_z(slot // GROUP, sign)
         py = (y_lo + (slot // CORE) % Y_LO) % Y_LO
         pc = (core + slot) % CORE
         return pz * GROUP + py * CORE + pc
@@ -102,104 +103,117 @@
         column_of((mask_ref[pl.ds(clip, 1), :] == 0).astype(WIDE), tok) for clip in range(CLIPS)
     ]
 
-    def pack_kv(clip):
+    def send_kv(clip):
         for stream in range(4):
             load(clip, stream).wait()
 
-        def one(head, carry):
-            lanes = pl.ds(pl.multiple_of(head * d, d), d)
+        def one(slot, carry):
+            peer = seq_peer(slot, 1)
+            lanes = pl.ds(pl.multiple_of(peer * d, d), d)
             for stream in range(4):
                 part = raw[clip, stream, :, lanes]
                 if stream % 2:
                     part = (part.astype(WIDE) * live[clip]).astype(NARROW)
-                kvsend[clip, head, :, stream * d : (stream + 1) * d] = part
+                kvsend[clip, peer, :, stream * d : (stream + 1) * d] = part
+
+            @pl.when(slot != 0)
+            def _():
+                pltpu.make_async_remote_copy(
+                    src_ref=kvsend.at[clip, peer],
+                    dst_ref=kvbuf.at[clip, pl.ds(pl.multiple_of(slot * tok, tok), tok)],
+                    send_sem=kv_ss.at[clip],
+                    recv_sem=kv_rs.at[clip],
+                    device_id=device(peer, my_f),
+                ).start()
+
             return carry
 
         lax.fori_loop(0, n_seq, one, 0)
-
-    def pack_q(clip):
+        kvbuf[clip, :tok] = kvsend[clip, me]
+
+    def send_q(clip):
         for stream in range(4, 6):
             load(clip, stream).wait()
 
-        def one(head, carry):
-            lanes = pl.ds(pl.multiple_of(head * d, d), d)
-            part = raw[clip, 4, :, lanes]
-            qsend[clip, head, :, :d] = (part.astype(WIDE) * live[clip]).astype(NARROW)
-            qsend[clip, head, :, d:] = raw[clip, 5, :, lanes]
-            return carry
-
-        lax.fori_loop(0, n_seq, one, 0)
-
-    def send_kv(clip):
         def one(slot, carry):
             peer = seq_peer(slot, 1)
-            pltpu.make_async_remote_copy(
-                src_ref=kvsend.at[clip, peer],
-                dst_ref=kvbuf.at[clip, pl.ds(pl.multiple_of(slot * tok, tok), tok)],
-                send_sem=kv_ss.at[clip],
-                recv_sem=kv_rs.at[clip],
-                device_id=device(peer, my_f),
-            ).start()
+            lanes = pl.ds(pl.multiple_of(peer * d, d), d)
+            part = raw[clip, 4, :, lanes]
+            qsend[clip, peer, :, :d] = (part.astype(WIDE) * live[clip]).astype(NARROW)
+            qsend[clip, peer, :, d:] = raw[clip, 5, :, lanes]
+
+            @pl.when(slot != 0)
+            def _():
+                pltpu.make_async_remote_copy(
+                    src_ref=qsend.at[clip, peer],
+                    dst_ref=qbuf.at[clip, pl.ds(pl.multiple_of(slot * tok, tok), tok)],
+                    send_sem=q_ss.at[clip],
+                    recv_sem=q_rs.at[clip, slot // GROUP],
+                    device_id=device(peer, my_f),
+                ).start()
+
             return carry
 
-        lax.fori_loop(1, n_seq, one, 0)
-        kvbuf[clip, :tok] = kvsend[clip, me]
-
-    def send_q(clip):
-        def one(slot, carry):
-            peer = seq_peer(slot, 1)
-            pltpu.make_async_remote_copy(
-                src_ref=qsend.at[clip, peer],
-                dst_ref=qbuf.at[clip, pl.ds(pl.multiple_of(slot * tok, tok), tok)],
-                send_sem=q_ss.at[clip],
-                recv_sem=q_rs.at[clip, slot // GROUP],
-                device_id=device(peer, my_f),
-            ).start()
-            return carry
-
-        lax.fori_loop(1, n_seq, one, 0)
+        lax.fori_loop(0, n_seq, one, 0)
         qbuf[clip, :tok] = qsend[clip, me]
 
     def drain(ref, sem):
         pltpu.make_async_copy(ref, ref, sem).wait()
 
-    pack_kv(0)
     pl.semaphore_wait(barrier, n_seq - 1 + len(x_peers) + len(y_far))
 
-    own_weight.wait()
-    mine = wbuf.at[z, y_lo, core, y_hi, x]
-
     def spread_z(step, carry):
-        peer_z = (z + step) % n_z
         pltpu.make_async_remote_copy(
-            src_ref=mine, dst_ref=mine, send_sem=w_ss.at[0], recv_sem=w_rs.at[0],
-            device_id=device(peer_z * GROUP + y_lo * CORE + core, my_f),
+            src_ref=weight_ref, dst_ref=wbuf.at[z, y_lo, core, y_hi, x],
+            send_sem=w_ss.at[0], recv_sem=w_rs.at[0, step],
+            device_id=device(ring_z(step, 1) * GROUP + y_lo * CORE + core, my_f),
         ).start()
         return carry
 
+    def spread_y(step):
+        part = wbuf.at[ring_z(step, -1), y_lo, core, y_hi, x]
+        for peer in y_peers:
+            pltpu.make_async_remote_copy(
+                src_ref=part, dst_ref=part, send_sem=w_ss.at[1], recv_sem=w_rs.at[1, step],
+                device_id=peer,
+            ).start()
+
+    def spread_x(step):
+        drain(wbuf.at[0, 0, 0, 0, : len(y_peers)], w_rs.at[1, step])
+        part = wbuf.at[ring_z(step, -1), :, core, :, x]
+        for peer in x_peers:
+            pltpu.make_async_remote_copy(
+                src_ref=part, dst_ref=part, send_sem=w_ss.at[2], recv_sem=w_rs.at[2, step],
+                device_id=peer,
+            ).start()
+
+    def spread_core(step, carry):
+        drain(wbuf.at[0, :, 0, :, : n_x - 1], w_rs.at[2, step])
+        part = wbuf.at[ring_z(step, -1), :, core]
+        pltpu.make_async_remote_copy(
+            src_ref=part, dst_ref=part, send_sem=w_ss.at[3], recv_sem=w_rs.at[3, step],
+            device_id=device(z * GROUP + y_lo * CORE + (core + 1) % CORE, my_f),
+        ).start()
+        return carry
+
     lax.fori_loop(1, n_z, spread_z, 0)
+    own_weight.wait()
+    spread_y(0)
     send_kv(0)
-    pack_q(0)
     send_q(0)
-    pack_kv(1)
     send_kv(1)
-    pack_q(1)
     send_q(1)
     for copy in late_loads:
         copy.start()
 
-    drain(wbuf.at[: n_z - 1, 0, 0, 0, 0], w_rs.at[0])
-    for peer in y_peers:
-        part = wbuf.at[:, y_lo, core, y_hi, x]
-        pltpu.make_async_remote_copy(
-            src_ref=part, dst_ref=part, send_sem=w_ss.at[1], recv_sem=w_rs.at[1], device_id=peer
-        ).start()
-    drain(wbuf.at[:, 0, 0, 0, : len(y_peers)], w_rs.at[1])
-    for peer in x_peers:
-        part = wbuf.at[:, :, core, :, x]
-        pltpu.make_async_remote_copy(
-            src_ref=part, dst_ref=part, send_sem=w_ss.at[2], recv_sem=w_rs.at[2], device_id=peer
-        ).start()
+    def spread_yx(step, carry):
+        drain(wbuf.at[0, 0, 0, 0, 0], w_rs.at[0, step])
+        spread_y(step)
+        spread_x(step - 1)
+        return carry
+
+    lax.fori_loop(1, n_z, spread_yx, 0)
+    spread_x(n_z - 1)
 
     scale = d ** (-0.5)
     to_exponent = scale * math.log2(math.e)
@@ -274,14 +288,15 @@
         orecv[clip, me] = osend[clip, 0]
 
     attend(0)
-    drain(wbuf.at[:, :, 0, :, : n_x - 1], w_rs.at[2])
-    part = wbuf.at[:, :, core]
-    pltpu.make_async_remote_copy(
-        src_ref=part, dst_ref=part, send_sem=w_ss.at[3], recv_sem=w_rs.at[3],
-        device_id=device(z * GROUP + y_lo * CORE + (core + 1) % CORE, my_f),
-    ).start()
+    lax.fori_loop(0, EARLY_CHUNKS, spread_core, 0)
     attend(1)
-    drain(wbuf.at[:, :, 0], w_rs.at[3])
+    lax.fori_loop(EARLY_CHUNKS, n_z, spread_core, 0)
+
+    def settle(step, carry):
+        drain(wbuf.at[0, :, 0], w_rs.at[3, step])
+        return carry
+
+    lax.fori_loop(0, n_z, settle, 0)
     for copy in late_loads:
         copy.wait()
 
@@ -370,7 +385,7 @@
             pltpu.VMEM((2 * tok, width), NARROW),
             dma((clips, 6)), dma((4,)),
             dma((clips,)), dma((clips,)), dma((clips,)), dma((clips, n_z)), dma((clips,)), dma((clips,)),
-            dma((4,)), dma((4,)), dma((1,)),
+            dma((4,)), dma((4, n_z)), dma((1,)),
         ],
         compiler_params=pltpu.CompilerParams(
             collective_id=0, has_side_effects=True, vmem_limit_bytes=62 * 2**20

time: 265 us -> 220 us (0.83)
  Pallas kernels: 262 us -> 214 us
    pallas_call x1, Pallas kernels: 262 us -> 214 us  [body(): pl.pallas_call(functools.partial(kernel, (n_z, n_x, tok, n_out)), out_sha...]
where the time goes in v2:
time: 220 us; the launch traced here: 218 us
  Pallas kernels  214 us (97%)
  local copies, waits for them, and re-layouts  2.87 us (1%)
    pallas_call x1, Pallas kernels, body(): pl.pallas_call(functools.partial(kernel, (n_z, n_x, tok, n_out)), out_sha...  214 us

profile of v2, /device:TPU:1, one launch (start us, length us, event | category | flops | bytes accessed | tf_op | source)
XLA Modules:
  0.0 217.9 jit_solution(8725925747951899300)
XLA Ops:
  0.6 214.4 %shard_map.140 = (bf16[2,64,2560]{2,1,0:T(8,128)(2,1)}, bf16[2,64,2560]{2,1,0:T(8,128)(2,1)}) custom-call(bf16[2,64,4096]{2,1,0:T(8,128)(2,1)} %q_ref.1, bf16[2,64,4096]{2,1,0:T(8,128)(2,1)} %k_ref.1, bf16[2,64,4096]{2,1,0:T(8,128)(2,1)} %v_ref.1, bf16[2,64,4096]{2,1,0:T(8,128)(2,1)} %qt_ref.1, bf16[2,64,4096]{2,1,0:T(8,128)(2,1)} %kt_ref.1, ...), custom_call_target="tpu_custom_call" | custom-call | flops 20000000000 | bytes 12582912 | tf_op jit(solution)/shard_map/pallas_call | solution.py:366
  215.0 0.0 copy-start
  215.0 2.0 copy.17
  217.1 0.0 copy-done
  217.1 0.8 copy.18
Async XLA Ops:
  215.0 2.0 copy-start

commit v3 on v2

--- a/solution.py
+++ b/solution.py
@@ -29,7 +29,7 @@
     mask_ref, time_ref, gate_ref, slope_ref, weight_ref,
     out_ref, tan_ref,
     raw, kvsend, kvbuf, qsend, qbuf, osend, orecv, wbuf, resbuf, gatebuf,
-    scores, probs, sums, joined,
+    scores, probs, sums, joined, total,
     load_sem, res_sem, kv_ss, kv_rs, q_ss, q_rs, o_ss, o_rs, w_ss, w_rs, own_sem,
 ):
     n_z, n_x, tok, n_out = dims
@@ -47,10 +47,13 @@
         return (z + (2 * (step % 2) - 1) * ((step + 1) // 2) * sign + n_z) % n_z
 
     def seq_peer(slot, sign):
-        pz = ring_z(slot // GROUP, sign)
+        pz = ring_z(n_z - 1 - slot // GROUP, sign)
         py = (y_lo + (slot // CORE) % Y_LO) % Y_LO
         pc = (core + slot) % CORE
         return pz * GROUP + py * CORE + pc
+
+    own_slot = (n_z - 1) * GROUP
+    own_rows = slice(own_slot * tok, (own_slot + 1) * tok)
 
     def device(seq, fsdp):
         return {"seq": seq, "fsdp": fsdp}
@@ -91,8 +94,8 @@
 
     barrier = pltpu.get_barrier_semaphore()
 
-    def greet(slot, carry):
-        pl.semaphore_signal(barrier, inc=1, device_id=device(seq_peer(slot, 1), my_f))
+    def greet(step, carry):
+        pl.semaphore_signal(barrier, inc=1, device_id=device((me + step) % n_seq, my_f))
         return carry
 
     lax.fori_loop(1, n_seq, greet, 0)
@@ -103,10 +106,11 @@
         column_of((mask_ref[pl.ds(clip, 1), :] == 0).astype(WIDE), tok) for clip in range(CLIPS)
     ]
 
-    def send_kv(clip):
+    def await_kv(clip):
         for stream in range(4):
             load(clip, stream).wait()
 
+    def send_kv(clip, first, last):
         def one(slot, carry):
             peer = seq_peer(slot, 1)
             lanes = pl.ds(pl.multiple_of(peer * d, d), d)
@@ -116,7 +120,7 @@
                     part = (part.astype(WIDE) * live[clip]).astype(NARROW)
                 kvsend[clip, peer, :, stream * d : (stream + 1) * d] = part
 
-            @pl.when(slot != 0)
+            @pl.when(slot != own_slot)
             def _():
                 pltpu.make_async_remote_copy(
                     src_ref=kvsend.at[clip, peer],
@@ -128,8 +132,9 @@
 
             return carry
 
-        lax.fori_loop(0, n_seq, one, 0)
-        kvbuf[clip, :tok] = kvsend[clip, me]
+        lax.fori_loop(first, last, one, 0)
+        if last == n_seq:
+            kvbuf[clip, own_rows] = kvsend[clip, me]
 
     def send_q(clip):
         for stream in range(4, 6):
@@ -142,7 +147,7 @@
             qsend[clip, peer, :, :d] = (part.astype(WIDE) * live[clip]).astype(NARROW)
             qsend[clip, peer, :, d:] = raw[clip, 5, :, lanes]
 
-            @pl.when(slot != 0)
+            @pl.when(slot != own_slot)
             def _():
                 pltpu.make_async_remote_copy(
                     src_ref=qsend.at[clip, peer],
@@ -155,20 +160,29 @@
             return carry
 
         lax.fori_loop(0, n_seq, one, 0)
-        qbuf[clip, :tok] = qsend[clip, me]
+        qbuf[clip, own_rows] = qsend[clip, me]
 
     def drain(ref, sem):
         pltpu.make_async_copy(ref, ref, sem).wait()
 
     pl.semaphore_wait(barrier, n_seq - 1 + len(x_peers) + len(y_far))
 
-    def spread_z(step, carry):
+    def to_neighbour(sign, part, step):
         pltpu.make_async_remote_copy(
-            src_ref=weight_ref, dst_ref=wbuf.at[z, y_lo, core, y_hi, x],
-            send_sem=w_ss.at[0], recv_sem=w_rs.at[0, step],
-            device_id=device(ring_z(step, 1) * GROUP + y_lo * CORE + core, my_f),
+            src_ref=part, dst_ref=part, send_sem=w_ss.at[0], recv_sem=w_rs.at[0, step],
+            device_id=device(ring_z(1, sign) * GROUP + y_lo * CORE + core, my_f),
         ).start()
-        return carry
+
+    def relay(far):
+        for side, sign in ((2 * far - 1, 1), (2 * far, -1)):
+            part = wbuf.at[ring_z(side, -1), y_lo, core, y_hi, x]
+            drain(part, w_rs.at[0, side])
+            if 2 * far + 2 < n_z:
+                to_neighbour(sign, part, side + 2)
+            else:
+                half = part.shape[1] // 2
+                lanes = slice(0, half) if sign == 1 else slice(half, 2 * half)
+                to_neighbour(sign, part.at[:, lanes], 2 * far + 1)
 
     def spread_y(step):
         part = wbuf.at[ring_z(step, -1), y_lo, core, y_hi, x]
@@ -196,43 +210,72 @@
         ).start()
         return carry
 
-    lax.fori_loop(1, n_z, spread_z, 0)
     own_weight.wait()
+    mine = wbuf.at[z, y_lo, core, y_hi, x]
+    to_neighbour(1, mine, 1)
+    to_neighbour(-1, mine, 2)
     spread_y(0)
-    send_kv(0)
+    await_kv(0)
+    hops = n_z // 2
+    send_kv(0, 0, GROUP)
+    for far in range(1, hops):
+        relay(far)
+        spread_y(2 * far - 1)
+        spread_y(2 * far)
+        for step in range(max(2 * far - 5, 0), 2 * far - 3):
+            spread_x(step)
+        send_kv(0, (2 * far - 1) * GROUP, (2 * far + 1) * GROUP)
+    send_kv(0, (n_z - 1) * GROUP, n_seq)
+    drain(wbuf.at[0, 0, 0, 0, 0], w_rs.at[0, n_z - 1])
+    spread_y(n_z - 1)
     send_q(0)
-    send_kv(1)
+
+    def continue_x(step, carry):
+        spread_x(step)
+        return carry
+
+    lax.fori_loop(n_z - 5, n_z, continue_x, 0)
+    await_kv(1)
+    send_kv(1, 0, n_seq)
     send_q(1)
     for copy in late_loads:
         copy.start()
 
-    def spread_yx(step, carry):
-        drain(wbuf.at[0, 0, 0, 0, 0], w_rs.at[0, step])
-        spread_y(step)
-        spread_x(step - 1)
-        return carry
-
-    lax.fori_loop(1, n_z, spread_yx, 0)
-    spread_x(n_z - 1)
-
     scale = d ** (-0.5)
     to_exponent = scale * math.log2(math.e)
     step_rows = 16
 
+    def give_back(clip, index):
+        for part in range(GROUP):
+            slot = index * GROUP + part
+            copy = pltpu.make_async_remote_copy(
+                src_ref=osend.at[clip, slot],
+                dst_ref=orecv.at[clip, me],
+                send_sem=o_ss.at[clip],
+                recv_sem=o_rs.at[clip, index],
+                device_id=device(seq_peer(slot, -1), my_f),
+            )
+            if part:
+                copy.start()
+            else:
+                pl.when(index != n_z - 1)(copy.start)
+
     def attend(clip):
         drain(kvbuf.at[clip, tok:], kv_rs.at[clip])
 
         def block(index, carry):
             start = pl.multiple_of(index * rows, rows)
 
-            @pl.when(index == 0)
-            def _():
-                drain(qbuf.at[clip, tok:rows], q_rs.at[clip, 0])
-
-            @pl.when(index != 0)
-            def _():
-                drain(qbuf.at[clip, pl.ds(start, rows)], q_rs.at[clip, index])
-
+            @pl.when(index == n_z - 1)
+            def _():
+                drain(qbuf.at[clip, tok:rows], q_rs.at[clip, index])
+
+            @pl.when(index != n_z - 1)
+            def _():
+                drain(qbuf.at[clip, :rows], q_rs.at[clip, index])
+
+            if clip:
+                give_back(clip - 1, index)
             both = qbuf[clip, pl.ds(start, rows)]
             plain = both[:, d:]
             left = jnp.concatenate(
@@ -247,15 +290,15 @@
                 at = pl.multiple_of(step * step_rows, step_rows)
                 exponent = scores[pl.ds(at, step_rows)] * to_exponent
                 weight = jnp.exp2(exponent - jnp.max(exponent, 1, keepdims=True))
-                total = jnp.sum(weight, 1, keepdims=True)
+                norm = jnp.sum(weight, 1, keepdims=True)
                 slant = scores[pl.ds(rows + at, step_rows)]
-                centre = jnp.sum(weight * slant, 1, keepdims=True) / total
+                centre = jnp.sum(weight * slant, 1, keepdims=True) / norm
                 probs[pl.ds(at, step_rows)] = weight.astype(NARROW)
                 probs[pl.ds(rows + at, step_rows)] = (weight * (slant - centre)).astype(NARROW)
-                sums[pl.ds(at, step_rows)] = jnp.broadcast_to(1.0 / total, (step_rows, d))
+                sums[pl.ds(at, step_rows)] = jnp.broadcast_to(1.0 / norm, (step_rows, d))
                 return carry
 
-            lax.fori_loop(0, rows // step_rows, soften, 0)
+            lax.fori_loop(0, rows // step_rows, soften, 0, unroll=4)
             result = jnp.dot(
                 probs[...], kvbuf[clip, :, 2 * d :], preferred_element_type=WIDE
             )
@@ -269,23 +312,12 @@
                 at = slice(part * tok, (part + 1) * tok)
                 osend[clip, slot, :tok] = value[at]
                 osend[clip, slot, tok:] = value_tan[at]
-            for part in range(GROUP):
-                slot = index * GROUP + part
-                copy = pltpu.make_async_remote_copy(
-                    src_ref=osend.at[clip, slot],
-                    dst_ref=orecv.at[clip, me],
-                    send_sem=o_ss.at[clip],
-                    recv_sem=o_rs.at[clip],
-                    device_id=device(seq_peer(slot, -1), my_f),
-                )
-                if part:
-                    copy.start()
-                else:
-                    pl.when(index != 0)(copy.start)
+            if clip == CLIPS - 1:
+                give_back(clip, index)
             return carry
 
         lax.fori_loop(0, n_z, block, 0)
-        orecv[clip, me] = osend[clip, 0]
+        orecv[clip, me] = osend[clip, own_slot]
 
     attend(0)
     lax.fori_loop(0, EARLY_CHUNKS, spread_core, 0)
@@ -300,36 +332,72 @@
     for copy in late_loads:
         copy.wait()
 
-    tile = 256
+    tile = 512
+    depth = GROUP * d
     steps = gatebuf.shape[1]
 
-    def project(clip):
-        drain(orecv.at[clip, : n_seq - 1], o_rs.at[clip])
-        for head in range(n_seq):
-            joined[:, head * d : (head + 1) * d] = orecv[clip, head]
-        picked = (
-            lax.broadcasted_iota(jnp.int32, (steps, 1), 0) == time_ref[clip]
-        ).astype(WIDE)
+    picked = [
+        (lax.broadcasted_iota(jnp.int32, (steps, 1), 0) == time_ref[clip]).astype(WIDE)
+        for clip in range(CLIPS)
+    ]
+
+    def gather(step):
+        at = ring_z(n_z - 1 - step, 1)
+        for clip in range(CLIPS):
+            for part in range(GROUP):
+                joined[clip * 2 * tok : (clip + 1) * 2 * tok, part * d : (part + 1) * d] = orecv[
+                    clip, at * GROUP + part
+                ]
+        return at
+
+    def product(at, index):
+        lanes = pl.ds(pl.multiple_of(index * tile, tile), tile)
+        weight = wbuf[at, :, :, :, :, :, lanes].reshape(depth, tile)
+        return lanes, jnp.dot(joined[...], weight, preferred_element_type=WIDE)
+
+    def project(step, carry):
+        for clip in range(CLIPS):
+            drain(orecv.at[clip, :GROUP], o_rs.at[clip, step])
+        at = gather(step)
 
         def one(index, carry):
-            lanes = pl.ds(pl.multiple_of(index * tile, tile), tile)
-            weight = wbuf[:, :, :, :, :, :, lanes].reshape(n_seq * d, tile)
-            both = jnp.dot(joined[...], weight, preferred_element_type=WIDE)
-            gate = jnp.sum(gatebuf[0, :, lanes] * picked, 0, keepdims=True)
-            slope = jnp.sum(gatebuf[1, :, lanes] * picked, 0, keepdims=True)
-            plain, tangent = both[:tok], both[tok:]
+            lanes, both = product(at, index)
+
+            @pl.when(step == 0)
+            def _():
+                total[:, lanes] = both
+
+            @pl.when(step != 0)
+            def _():
+                total[:, lanes] += both
+
+            return carry
+
+        lax.fori_loop(0, n_out // tile, one, 0, unroll=True)
+        return carry
+
+    lax.fori_loop(0, n_z - 1, project, 0)
+    for clip in range(CLIPS):
+        drain(orecv.at[clip, : GROUP - 1], o_rs.at[clip, n_z - 1])
+    nearest = gather(n_z - 1)
+
+    def finish(index, carry):
+        lanes, both = product(nearest, index)
+        both = total[:, lanes] + both
+        for clip in range(CLIPS):
+            gate = jnp.sum(gatebuf[0, :, lanes] * picked[clip], 0, keepdims=True)
+            slope = jnp.sum(gatebuf[1, :, lanes] * picked[clip], 0, keepdims=True)
+            at = clip * 2 * tok
+            plain, tangent = both[at : at + tok], both[at + tok : at + 2 * tok]
             out_ref[clip, :, lanes] = (
                 resbuf[0, clip, :, lanes].astype(WIDE) + gate * plain
             ).astype(NARROW)
             tan_ref[clip, :, lanes] = (
                 resbuf[1, clip, :, lanes].astype(WIDE) * live[clip] + slope * plain + gate * tangent
             ).astype(NARROW)
-            return carry
-
-        lax.fori_loop(0, n_out // tile, one, 0)
-
-    project(0)
-    project(1)
+        return carry
+
+    lax.fori_loop(0, n_out // tile, finish, 0, unroll=True)
 
     for clip in range(CLIPS):
         drain(kvsend.at[clip, : n_seq - 1], kv_ss.at[clip])
@@ -382,9 +450,10 @@
             pltpu.VMEM((2 * rows, length), WIDE),
             pltpu.VMEM((2 * rows, length), NARROW),
             pltpu.VMEM((rows, d), WIDE),
-            pltpu.VMEM((2 * tok, width), NARROW),
+            pltpu.VMEM((clips * 2 * tok, GROUP * d), NARROW),
+            pltpu.VMEM((clips * 2 * tok, n_out), WIDE),
             dma((clips, 6)), dma((4,)),
-            dma((clips,)), dma((clips,)), dma((clips,)), dma((clips, n_z)), dma((clips,)), dma((clips,)),
+            dma((clips,)), dma((clips,)), dma((clips,)), dma((clips, n_z)), dma((clips,)), dma((clips, n_z)),
             dma((4,)), dma((4, n_z)), dma((1,)),
         ],
         compiler_params=pltpu.CompilerParams(

time: 220 us -> 209 us (0.950); the launches traced: 218 us -> 209 us
  Pallas kernels: 214 us -> 206 us
    pallas_call x1, Pallas kernels: 214 us -> 206 us  [body(): pl.pallas_call(functools.partial(kernel, (n_z, n_x, tok, n_out)), out_sha...]
where the time goes in v3:
time: 209 us
  Pallas kernels  206 us (99%)
  local copies, waits for them, and re-layouts  2.87 us (1%)
    pallas_call x1, Pallas kernels, body(): pl.pallas_call(functools.partial(kernel, (n_z, n_x, tok, n_out)), out_sha...  206 us

profile of v3, /device:TPU:1, one launch (start us, length us, event | category | flops | bytes accessed | tf_op | source)
XLA Modules:
  0.0 209.2 jit_solution(3586750728718127602)
XLA Ops:
  0.6 205.7 %shard_map.140 = (bf16[2,64,2560]{2,1,0:T(8,128)(2,1)}, bf16[2,64,2560]{2,1,0:T(8,128)(2,1)}) custom-call(bf16[2,64,4096]{2,1,0:T(8,128)(2,1)} %q_ref.1, bf16[2,64,4096]{2,1,0:T(8,128)(2,1)} %k_ref.1, bf16[2,64,4096]{2,1,0:T(8,128)(2,1)} %v_ref.1, bf16[2,64,4096]{2,1,0:T(8,128)(2,1)} %qt_ref.1, bf16[2,64,4096]{2,1,0:T(8,128)(2,1)} %kt_ref.1, ...), custom_call_target="tpu_custom_call" | custom-call | flops 20000000000 | bytes 12582912 | tf_op jit(solution)/shard_map/pallas_call | solution.py:434
  206.3 0.0 copy-start
  206.3 2.0 copy.17
  208.3 0.0 copy-done
  208.3 0.8 copy.18
Async XLA Ops:
  206.3 2.0 copy-start

commit v4 on v3

--- a/solution.py
+++ b/solution.py
@@ -29,8 +29,8 @@
     mask_ref, time_ref, gate_ref, slope_ref, weight_ref,
     out_ref, tan_ref,
     raw, kvsend, kvbuf, qsend, qbuf, osend, orecv, wbuf, resbuf, gatebuf,
-    scores, probs, sums, joined, total,
-    load_sem, res_sem, kv_ss, kv_rs, q_ss, q_rs, o_ss, o_rs, w_ss, w_rs, own_sem,
+    scores, probs, sums, joined, total, outbuf,
+    load_sem, res_sem, kv_ss, kv_rs, q_ss, q_rs, o_ss, o_rs, w_ss, w_rs, own_sem, store_sem,
 ):
     n_z, n_x, tok, n_out = dims
     n_seq = n_z * GROUP
@@ -73,6 +73,16 @@
         [(b, a) for b in range(y_hi_count) for a in range(Y_LO) if (a, b) != (0, 0)],
     ) if b]
 
+    barrier = pltpu.get_barrier_semaphore()
+
+    def greet(step, carry):
+        pl.semaphore_signal(barrier, inc=1, device_id=device((me + step) % n_seq, my_f))
+        return carry
+
+    lax.fori_loop(1, n_seq, greet, 0)
+    for peer in x_peers + y_far:
+        pl.semaphore_signal(barrier, inc=1, device_id=peer)
+
     streams = (k_ref, kt_ref, v_ref, vt_ref, qt_ref, q_ref)
 
     def load(clip, stream):
@@ -91,16 +101,6 @@
         pltpu.make_async_copy(gate_ref, gatebuf.at[0], res_sem.at[2]),
         pltpu.make_async_copy(slope_ref, gatebuf.at[1], res_sem.at[3]),
     ]
-
-    barrier = pltpu.get_barrier_semaphore()
-
-    def greet(step, carry):
-        pl.semaphore_signal(barrier, inc=1, device_id=device((me + step) % n_seq, my_f))
-        return carry
-
-    lax.fori_loop(1, n_seq, greet, 0)
-    for peer in x_peers + y_far:
-        pl.semaphore_signal(barrier, inc=1, device_id=peer)
 
     live = [
         column_of((mask_ref[pl.ds(clip, 1), :] == 0).astype(WIDE), tok) for clip in range(CLIPS)
@@ -381,6 +381,12 @@
         drain(orecv.at[clip, : GROUP - 1], o_rs.at[clip, n_z - 1])
     nearest = gather(n_z - 1)
 
+    def store(which, lanes):
+        return pltpu.make_async_copy(
+            outbuf.at[which, :, :, lanes], (out_ref, tan_ref)[which].at[:, :, lanes],
+            store_sem.at[which],
+        )
+
     def finish(index, carry):
         lanes, both = product(nearest, index)
         both = total[:, lanes] + both
@@ -389,15 +395,19 @@
             slope = jnp.sum(gatebuf[1, :, lanes] * picked[clip], 0, keepdims=True)
             at = clip * 2 * tok
             plain, tangent = both[at : at + tok], both[at + tok : at + 2 * tok]
-            out_ref[clip, :, lanes] = (
+            outbuf[0, clip, :, lanes] = (
                 resbuf[0, clip, :, lanes].astype(WIDE) + gate * plain
             ).astype(NARROW)
-            tan_ref[clip, :, lanes] = (
+            outbuf[1, clip, :, lanes] = (
                 resbuf[1, clip, :, lanes].astype(WIDE) * live[clip] + slope * plain + gate * tangent
             ).astype(NARROW)
+        for which in range(2):
+            store(which, lanes).start()
         return carry
 
     lax.fori_loop(0, n_out // tile, finish, 0, unroll=True)
+    for which in range(2):
+        drain(outbuf.at[which], store_sem.at[which])
 
     for clip in range(CLIPS):
         drain(kvsend.at[clip, : n_seq - 1], kv_ss.at[clip])
@@ -435,7 +445,7 @@
         functools.partial(kernel, (n_z, n_x, tok, n_out)),
         out_shape=(out_shape, out_shape),
         in_specs=[anywhere] * 8 + [vmem, smem] + [anywhere] * 3,
-        out_specs=(vmem, vmem),
+        out_specs=(anywhere, anywhere),
         scratch_shapes=[
             pltpu.VMEM((clips, 6, tok, width), NARROW),
             pltpu.VMEM((clips, n_seq, tok, 4 * d), NARROW),
@@ -452,9 +462,10 @@
             pltpu.VMEM((rows, d), WIDE),
             pltpu.VMEM((clips * 2 * tok, GROUP * d), NARROW),
             pltpu.VMEM((clips * 2 * tok, n_out), WIDE),
+            pltpu.VMEM((2, clips, tok, n_out), NARROW),
             dma((clips, 6)), dma((4,)),
             dma((clips,)), dma((clips,)), dma((clips,)), dma((clips, n_z)), dma((clips,)), dma((clips, n_z)),
-            dma((4,)), dma((4, n_z)), dma((1,)),
+            dma((4,)), dma((4, n_z)), dma((1,)), dma((2,)),
         ],
         compiler_params=pltpu.CompilerParams(
             collective_id=0, has_side_effects=True, vmem_limit_bytes=62 * 2**20

time: 209 us -> 209 us (level)
  no operation moved by 1% of the time
where the time goes in v4:
time: 209 us
  Pallas kernels  205 us (98%)
  local copies, waits for them, and re-layouts  2.87 us (1%)
    pallas_call x1, Pallas kernels, body(): pl.pallas_call(functools.partial(kernel, (n_z, n_x, tok, n_out)), out_sha...  205 us

profile of v4, /device:TPU:1, one launch (start us, length us, event | category | flops | bytes accessed | tf_op | source)
XLA Modules:
  0.0 208.9 jit_solution(10742275427400727075)
XLA Ops:
  0.6 205.4 %shard_map.140 = (bf16[2,64,2560]{2,1,0:T(8,128)(2,1)}, bf16[2,64,2560]{2,1,0:T(8,128)(2,1)}) custom-call(bf16[2,64,4096]{2,1,0:T(8,128)(2,1)} %q_ref.1, bf16[2,64,4096]{2,1,0:T(8,128)(2,1)} %k_ref.1, bf16[2,64,4096]{2,1,0:T(8,128)(2,1)} %v_ref.1, bf16[2,64,4096]{2,1,0:T(8,128)(2,1)} %qt_ref.1, bf16[2,64,4096]{2,1,0:T(8,128)(2,1)} %kt_ref.1, ...), custom_call_target="tpu_custom_call" | custom-call | flops 20000000000 | bytes 12582912 | tf_op jit(solution)/shard_map/pallas_call | solution.py:444
  206.0 0.0 copy-start
  206.0 2.0 copy.17
  208.0 0.0 copy-done
  208.0 0.8 copy.18
Async XLA Ops:
  206.0 2.0 copy-start
